TPU v7x, 512 devices: a whole 4x4x16 slice. The times are simulated.
512 devices in a mesh: gx: 64 (over z, x), gy: 8 (over y, core).
Axes of the slice: x: 4, y: 4, z: 16, core: 2. Of those that a mesh axis runs over, the one named last changes fastest.
Arguments:
- object_field: float32 [2, 2, 1024, 16384], P(None, None, 'gy', 'gx'), may hold values from -5 to 5
- first_moment: float32 [2, 2, 1024, 16384], P(None, None, 'gy', 'gx'), may hold values from -2 to 2
- second_moment: float32 [2, 2, 1024, 16384], P(None, None, 'gy', 'gx'), may hold values from 0.2 to 4
- probe_wave: float32 [2, 128, 128], replicated, may hold values from -5 to 5
- patterns: float32 [8, 768, 128, 128], P('gy', 'gx'), may hold values from 0.05 to 5
- row_offsets: int32 [8, 768], P('gy', 'gx'), may hold values from 0 to 127
- col_offsets: int32 [8, 768], P('gy', 'gx'), may hold values from 0 to 255
- counts: int32 [8, 64], P('gy', 'gx'), may hold values from 1 to 12, as said below
Outputs:
- new_object: float32 [2, 2, 1024, 16384], P(None, None, 'gy', 'gx')
- new_first: float32 [2, 2, 1024, 16384], P(None, None, 'gy', 'gx')
- new_second: float32 [2, 2, 1024, 16384], P(None, None, 'gy', 'gx')
Inputs may be any that keep to these rules, and one draw needn't show every extreme that they name: `counts`: every tile has 1 to 12 live slots and some tile has exactly 12; tiles (2 * c, b) and (2 * c + 1, b) have at most 16 live slots together, and some such pair has exactly that many.
All inputs are finite; a program needn't handle non-finite values.
Results may differ from a plain program's by a relative error of at most 0.0003.
Values sent between devices are 32-bit elements; how exact they have to be, the bound alone decides.
No kernel may reach another device: no remote copies, remote signals or barrier semaphores. Data moves between devices by JAX's collectives and lax.ppermute only.
A program may use at most 64 MiB of HBM per device.

v0:
```python
import functools
import math

import jax
import jax.numpy as jnp
import ml_dtypes
import numpy as np
from jax import lax
from jax.experimental import pallas as pl
from jax.experimental.pallas import tpu as pltpu
from jax.sharding import PartitionSpec as P

smoothing = 0.15
beta_first = 0.9
beta_second = 0.999
first_fix = 1.0 - 0.9**2
second_fix = 1.0 - 0.999**2
rate_scale = 0.25 * 1.2732395
misfit_weight = 1.0 / 64.0

W = 128
BATCH = 4
f32 = jnp.float32
bf16 = jnp.bfloat16
VMEM = pl.BlockSpec(memory_space=pltpu.VMEM)
SMEM = pl.BlockSpec(memory_space=pltpu.SMEM)


def embedded(matrix):
    return np.block([[matrix.real, matrix.imag], [-matrix.imag, matrix.real]])


def wave_tables():
    index = np.arange(W)
    angle = 2.0 * math.pi / W * (index[:, None] * index[None, :] % W)
    dft = (np.cos(angle) - 1j * np.sin(angle)) / math.sqrt(W)
    frequency = np.where(index < W // 2, index, index - W)
    hop = np.conj(dft) @ (np.exp(-1j * math.pi / 512.0 * frequency**2)[:, None] * dft)
    whole = np.stack([embedded(m) for m in (dft, np.conj(dft), hop, np.conj(hop))])
    high = whole.astype(ml_dtypes.bfloat16)
    low = (whole - high.astype(np.float64)).astype(ml_dtypes.bfloat16)
    return np.stack([high, low], axis=1)


DFT, DFT_CONJ, HOP, HOP_CONJ = range(4)
CONJ = (DFT_CONJ, DFT, HOP_CONJ, HOP)


def halves(values):
    high = values.astype(bf16)
    return high, (values - high.astype(f32)).astype(bf16)


def dot(a, b):
    return jnp.dot(a, b, preferred_element_type=f32)


def both_sides(waves, table, which):
    left = CONJ[which]
    columns = jnp.concatenate(
        [
            jnp.concatenate([re for re, im in waves], axis=1),
            jnp.concatenate([im for re, im in waves], axis=1),
        ],
        axis=0,
    )
    high, low = halves(columns)
    columns = dot(table[left, 0], high) + dot(table[left, 1], high) + dot(table[left, 0], low)
    rows = jnp.concatenate(
        [
            jnp.concatenate(
                [columns[:W, k * W : (k + 1) * W], columns[W:, k * W : (k + 1) * W]], axis=1
            )
            for k in range(len(waves))
        ],
        axis=0,
    )
    high, low = halves(rows)
    rows = dot(high, table[which, 0]) + dot(high, table[which, 1]) + dot(low, table[which, 0])
    return [
        (rows[k * W : (k + 1) * W, :W], rows[k * W : (k + 1) * W, W:]) for k in range(len(waves))
    ]


def times(a, b):
    return a[0] * b[0] - a[1] * b[1], a[0] * b[1] + a[1] * b[0]


def times_conj(a, b):
    return a[0] * b[0] + a[1] * b[1], a[1] * b[0] - a[0] * b[1]


def gradient_kernel(
    rows_ref,
    cols_ref,
    count_ref,
    edge_ref,
    here_ref,
    below_ref,
    right_ref,
    corner_ref,
    probe_ref,
    patterns_ref,
    table_ref,
    own_ref,
    down_ref,
    up_ref,
    side_ref,
    left_ref,
    obj,
    acc,
):
    for p in range(4):
        for t in range(2):
            obj[t, p, :W, :] = here_ref[p, :, t * W : (t + 1) * W]
            obj[t, p, W:, :] = below_ref[p, :, t * W : (t + 1) * W]
        obj[2, p, :W, :] = right_ref[p]
        obj[2, p, W:, :] = corner_ref[p]
    acc[...] = jnp.zeros_like(acc)
    lane = lax.broadcasted_iota(jnp.int32, (W, W), 1)
    count = count_ref[0, 0]

    def batch(step, carry):
        slots = [step * BATCH + j for j in range(BATCH)]
        places = []
        for k in slots:
            col = cols_ref[0, k]
            places.append((rows_ref[0, k], col // W, col % W))
        windows = []
        for row, tile, shift in places:
            planes = []
            for p in range(4):
                first = obj[tile, p, pl.ds(row, W), :]
                second = obj[tile + 1, p, pl.ds(row, W), :]
                chosen = jnp.where(lane >= shift, first, second)
                planes.append(pltpu.roll(chosen, (W - shift) % W, 1))
            windows.append(((planes[0], planes[2]), (planes[1], planes[3])))
        probe = (probe_ref[0], probe_ref[1])
        waves = [times(probe, window[0]) for window in windows]
        waves = both_sides(waves, table_ref, HOP)
        fars = both_sides([times(w, o[1]) for w, o in zip(waves, windows)], table_ref, DFT)
        back = []
        for k, far in zip(slots, fars):
            misfit = far[0] * far[0] + far[1] * far[1] - patterns_ref[k]
            misfit = misfit * jnp.where(k < count, 4.0 * misfit_weight, 0.0)
            back.append((misfit * far[0], misfit * far[1]))
        back = both_sides(back, table_ref, DFT_CONJ)
        second = [times_conj(g, w) for g, w in zip(back, waves)]
        back = both_sides([times_conj(g, o[1]) for g, o in zip(back, windows)], table_ref, HOP_CONJ)
        first = [times_conj(g, probe) for g in back]
        for (row, tile, shift), one, two in zip(places, first, second):
            for p, plane in enumerate((one[0], two[0], one[1], two[1])):
                turned = pltpu.roll(plane, shift, 1)
                at = pl.ds(row + 8, W)
                acc[tile, p, at, :] += jnp.where(lane >= shift, turned, 0.0)
                acc[tile + 1, p, at, :] += jnp.where(lane < shift, turned, 0.0)
        return carry

    lax.fori_loop(0, (count + BATCH - 1) // BATCH, batch, 0)

    @pl.when(edge_ref[0, 0] == 1)
    def _():
        acc[2] = jnp.zeros(acc.shape[1:], f32)

    @pl.when(edge_ref[0, 1] == 1)
    def _():
        acc[:, :, 8 + W :, :] = jnp.zeros((3, 4, acc.shape[2] - 8 - W, W), f32)

    lane = lax.broadcasted_iota(jnp.int32, (W, W), 1)
    down_ref[:, W:, :] = jnp.zeros((4, 8, 3 * W), f32)
    up_ref[...] = jnp.zeros_like(up_ref)
    left_ref[...] = jnp.zeros_like(left_ref)
    for p in range(4):
        for half in range(2):
            base = 8 + half * W
            centres = [acc[t, p, base : base + W, :] for t in range(3)]
            for t in range(3):
                above = acc[t, p, base - 1 : base - 1 + W, :]
                under = acc[t, p, base + 1 : base + 1 + W, :]
                before = pltpu.roll(centres[t], 1, 1)
                edge = pltpu.roll(centres[t - 1], 1, 1) if t else 0.0
                before = jnp.where(lane == 0, edge, before)
                after = pltpu.roll(centres[t], W - 1, 1)
                edge = pltpu.roll(centres[t + 1], W - 1, 1) if t < 2 else 0.0
                after = jnp.where(lane == W - 1, edge, after)
                smooth = centres[t] + smoothing * (
                    above + under + before + after - 4.0 * centres[t]
                )
                if half:
                    down_ref[p, :W, t * W : (t + 1) * W] = smooth
                elif t < 2:
                    own_ref[p, :, t * W : (t + 1) * W] = smooth
                else:
                    side_ref[p] = smooth
            rim = smoothing * centres[0].T[0:1, :]
            if half:
                down_ref[p, W : W + 1, :W] = rim
            else:
                left_ref[p : p + 1, :] = rim
        for t in range(3):
            up_ref[p : p + 1, t * W : (t + 1) * W] = smoothing * acc[t, p, 8:9, :]


def middle_kernel(side_ref, left_ref, above_ref, under_ref, side_out, left_out):
    for p in range(4):
        side_out[p] = side_ref[p] + above_ref[p, :W, 2 * W :]
        side_out[p, W - 1 : W, :] += under_ref[p : p + 1, 2 * W :]
    left_out[...] = left_ref[...]
    for p in range(4):
        left_out[p : p + 1, :] += above_ref[p, W : W + 1, :W]


def arc(slope):
    size = jnp.abs(slope)
    big = size > 2.414213562373095
    mid = size > 0.4142135623730950
    top = jnp.where(big, -1.0, jnp.where(mid, size - 1.0, size))
    low = jnp.where(big, size, jnp.where(mid, size + 1.0, 1.0))
    base = jnp.where(big, math.pi / 2, jnp.where(mid, math.pi / 4, 0.0))
    x = top / low
    z = x * x
    poly = (
        ((8.05374449538e-2 * z - 1.38776856032e-1) * z + 1.99777106478e-1) * z - 3.33329491539e-1
    ) * z * x + x
    value = base + poly
    return jnp.where(slope < 0.0, -value, value)


def update_kernel(
    obj_ref,
    first_ref,
    second_ref,
    own_ref,
    above_ref,
    under_ref,
    side_ref,
    left_ref,
    new_obj,
    new_first,
    new_second,
):
    row = lax.broadcasted_iota(jnp.int32, (W, W), 0)
    lane = lax.broadcasted_iota(jnp.int32, (W, W), 1)
    for p in range(4):
        for t in range(2):
            at = (p, slice(None), slice(t * W, (t + 1) * W))
            total = own_ref[at] + above_ref[p, :W, t * W : (t + 1) * W]
            total += jnp.where(row == W - 1, under_ref[p : p + 1, t * W : (t + 1) * W], 0.0)
            if t == 0:
                total += side_ref[p]
            else:
                column = jnp.broadcast_to(left_ref[p : p + 1, :], (W, W)).T
                total += jnp.where(lane == W - 1, column, 0.0)
            first = beta_first * first_ref[at] + (1.0 - beta_first) * total
            second = beta_second * second_ref[at] + (1.0 - beta_second) * total * total
            new_first[at] = first
            new_second[at] = second
            slope = (first * (1.0 / first_fix)) * lax.rsqrt(second * (1.0 / second_fix))
            new_obj[at] = obj_ref[at] - rate_scale * arc(slope)


def shift(block, axis, distance):
    count = lax.axis_size(axis)
    pairs = [(i + distance, i) for i in range(count) if 0 <= i + distance < count]
    return lax.ppermute(block, axis, pairs)


def call(kernel, outs, specs, scratch=()):
    return pl.pallas_call(
        kernel,
        out_shape=[jax.ShapeDtypeStruct(s, f32) for s in outs],
        in_specs=specs,
        out_specs=[VMEM] * len(outs),
        scratch_shapes=scratch,
        compiler_params=pltpu.CompilerParams(vmem_limit_bytes=40 * 1024 * 1024),
    )


def shards(
    object_field,
    first_moment,
    second_moment,
    probe_wave,
    patterns,
    row_offsets,
    col_offsets,
    counts,
    table,
):
    here = object_field.reshape(4, W, 2 * W)
    right = shift(here[:, :, :W], "gx", 1)
    below = shift(here, "gy", 1)
    corner = shift(right, "gy", 1)
    edge = jnp.stack(
        [
            lax.axis_index("gx") == lax.axis_size("gx") - 1,
            lax.axis_index("gy") == lax.axis_size("gy") - 1,
        ]
    ).astype(jnp.int32)[None]
    own, down, up, side, left = call(
        gradient_kernel,
        [(4, W, 2 * W), (4, W + 8, 3 * W), (8, 3 * W), (4, W, W), (8, W)],
        [SMEM] * 4 + [VMEM] * 7,
        [pltpu.VMEM((3, 4, 2 * W, W), f32), pltpu.VMEM((3, 4, 2 * W + 16, W), f32)],
    )(
        row_offsets,
        col_offsets,
        counts,
        edge,
        here,
        below,
        right,
        corner,
        probe_wave,
        patterns[0],
        table,
    )
    above = shift(down, "gy", -1)
    under = shift(up, "gy", 1)
    side, left = call(middle_kernel, [(4, W, W), (8, W)], [VMEM] * 4)(side, left, above, under)
    side = shift(side, "gx", -1)
    left = shift(left, "gx", 1)
    outs = call(update_kernel, [(4, W, 2 * W)] * 3, [VMEM] * 8)(
        here,
        first_moment.reshape(here.shape),
        second_moment.reshape(here.shape),
        own,
        above,
        under,
        side,
        left,
    )
    return tuple(out.reshape(object_field.shape) for out in outs)


def solution(mesh):
    whole = P(None, None, "gy", "gx")
    tiles = P("gy", "gx")
    body = jax.shard_map(
        shards,
        mesh=mesh,
        in_specs=(whole, whole, whole, P(), P("gy", "gx", None, None), tiles, tiles, tiles, P()),
        out_specs=(whole, whole, whole),
        check_vma=False,
    )

    def step(*args):
        return body(*args, jnp.asarray(wave_tables()))

    return step
```

profile of v0, /device:TPU:254, one launch (start us, length us, event | category | flops | bytes accessed | tf_op | source)
XLA Modules:
  0.0 63.8 jit_solution(4914233070367307483)
XLA Ops:
  0.6 0.0 copy-start
  0.6 1.0 %slice.4 = f32[4,128,128]{2,1,0:T(8,128)S(1)} slice(f32[4,128,256]{2,1,0:T(8,128)} %bitcast.9), slice={[0:4], [0:128], [0:128]} | slice | bytes 524288 | tf_op jit(solution)/shard_map/slice | solution.py:291
  1.7 2.7 %collective-permute-start.1 = (f32[4,128,128]{2,1,0:T(8,128)S(1)}, f32[4,128,128]{2,1,0:T(8,128)S(1)}, u32[]{:S(2)}, u32[]{:S(2)}) collective-permute-start(f32[4,128,128]{2,1,0:T(8,128)S(1)} %slice.4), channel_id=1, source_target_pairs={{8,0},{16,8},{24,16},{32,24},{40,32},{48,40},{56,48},{64,56},{72,6... | collective-permute-start | bytes 786440 | tf_op jit(solution)/shard_map/ppermute | solution.py:265
  4.4 0.0 copy-done
  4.4 1.9 %collective-permute-start = (f32[4,128,256]{2,1,0:T(8,128)S(1)}, f32[4,128,256]{2,1,0:T(8,128)S(1)}, u32[]{:S(2)}, u32[]{:S(2)}) collective-permute-start(f32[4,128,256]{2,1,0:T(8,128)S(1)} %bitcast.10), channel_id=1, source_target_pairs={{1,0},{2,1},{3,2},{4,3},{5,4},{6,5},{7,6},{9,8},{10,9},{11,10},{12... | collective-permute-start | bytes 1572872 | tf_op jit(solution)/shard_map/ppermute | solution.py:265
  6.4 8.6 %collective-permute-done.1.right_ref = f32[4,128,128]{2,1,0:T(8,128)S(1)} collective-permute-done((f32[4,128,128]{2,1,0:T(8,128)S(1)}, f32[4,128,128]{2,1,0:T(8,128)S(1)}, u32[]{:S(2)}, u32[]{:S(2)}) %collective-permute-start.1) | collective-permute-done | bytes 262176 | tf_op jit(solution)/shard_map/ppermute | solution.py:265
  14.9 1.9 %collective-permute-start.2 = (f32[4,128,128]{2,1,0:T(8,128)S(1)}, f32[4,128,128]{2,1,0:T(8,128)S(1)}, u32[]{:S(2)}, u32[]{:S(2)}) collective-permute-start(f32[4,128,128]{2,1,0:T(8,128)S(1)} %collective-permute-done.1.right_ref), channel_id=1, source_target_pairs={{1,0},{2,1},{3,2},{4,3},{5,4},{6,5},{7,6},{9,8},{10,9},{11,10},{12... | collective-permute-start | bytes 786440 | tf_op jit(solution)/shard_map/ppermute | solution.py:265
  17.5 0.1 add_convert_fusion.edge_ref
  17.6 3.1 %collective-permute-done.2.corner_ref = f32[4,128,128]{2,1,0:T(8,128)S(1)} collective-permute-done((f32[4,128,128]{2,1,0:T(8,128)S(1)}, f32[4,128,128]{2,1,0:T(8,128)S(1)}, u32[]{:S(2)}, u32[]{:S(2)}) %collective-permute-start.2) | collective-permute-done | bytes 262176 | tf_op jit(solution)/shard_map/ppermute | solution.py:265
  20.7 0.0 collective-permute-done.below_ref
  20.7 1.2 %copy-done.1 = bf16[4,2,256,256]{3,2,1,0:T(8,128)(2,1)S(1)} copy-done((bf16[4,2,256,256]{3,2,1,0:T(8,128)(2,1)S(1)}, bf16[4,2,256,256]{3,2,1,0:T(8,128)(2,1)}, u32[]{:S(2)}) %copy-start.1) | copy-done | bytes 1048600
  22.0 1.1 %copy-done.2 = f32[1,12,128,128]{3,2,1,0:T(8,128)S(1)} copy-done((f32[1,12,128,128]{3,2,1,0:T(8,128)S(1)}, f32[1,12,128,128]{3,2,1,0:T(8,128)}, u32[]{:S(2)}) %copy-start.2) | copy-done | bytes 786456
  23.1 0.9 %copy-done.5 = f32[2,128,128]{2,1,0:T(8,128)S(1)} copy-done((f32[2,128,128]{2,1,0:T(8,128)S(1)}, f32[2,128,128]{2,1,0:T(8,128)}, u32[]{:S(2)}) %copy-start.5) | copy-done | bytes 131096
  24.0 13.1 %shard_map.112 = (f32[4,128,256]{2,1,0:T(8,128)S(1)}, f32[4,136,384]{2,1,0:T(8,128)S(1)}, f32[8,384]{1,0:T(8,128)S(1)}, f32[4,128,128]{2,1,0:T(8,128)S(1)}, f32[8,128]{1,0:T(8,128)S(1)}) custom-call(s32[1,12]{1,0:T(1,128)S(1)} %copy-done.6, s32[1,12]{1,0:T(1,128)S(1)} %copy-done.7, s32[1,1]{1,0:T(1,128)S(6)} %copy.12.count_ref, ...), custom_call_target="tpu_custom_call" | custom-call | tf_op jit(solution)/shard_map/pallas_call | solution.py:300
  37.1 1.9 %collective-permute-start.3 = (f32[4,136,384]{2,1,0:T(8,128)S(1)}, f32[4,136,384]{2,1,0:T(8,128)S(1)}, u32[]{:S(2)}, u32[]{:S(2)}) collective-permute-start(f32[4,136,384]{2,1,0:T(8,128)S(1)} %get-tuple-element.14), channel_id=1, source_target_pairs={{0,1},{1,2},{2,3},{3,4},{4,5},{5,6},{6,7},{8,9},{9,10},{10,11},{11... | collective-permute-start | bytes 2506760 | tf_op jit(solution)/shard_map/ppermute | solution.py:265
  39.0 3.8 %collective-permute-start.4 = (f32[8,384]{1,0:T(8,128)S(1)}, f32[8,384]{1,0:T(8,128)S(1)}, u32[]{:S(2)}, u32[]{:S(2)}) collective-permute-start(f32[8,384]{1,0:T(8,128)S(1)} %get-tuple-element.15), channel_id=1, source_target_pairs={{1,0},{2,1},{3,2},{4,3},{5,4},{6,5},{7,6},{9,8},{10,9},{11,10},{12... | collective-permute-start | bytes 36872 | tf_op jit(solution)/shard_map/ppermute | solution.py:265
  42.9 1.4 %collective-permute-done.4.under_ref = f32[8,384]{1,0:T(8,128)S(1)} collective-permute-done((f32[8,384]{1,0:T(8,128)S(1)}, f32[8,384]{1,0:T(8,128)S(1)}, u32[]{:S(2)}, u32[]{:S(2)}) %collective-permute-start.4) | collective-permute-done | bytes 12320 | tf_op jit(solution)/shard_map/ppermute | solution.py:265
  44.3 6.9 %collective-permute-done.3.above_ref = f32[4,136,384]{2,1,0:T(8,128)S(1)} collective-permute-done((f32[4,136,384]{2,1,0:T(8,128)S(1)}, f32[4,136,384]{2,1,0:T(8,128)S(1)}, u32[]{:S(2)}, u32[]{:S(2)}) %collective-permute-start.3) | collective-permute-done | bytes 835616 | tf_op jit(solution)/shard_map/ppermute | solution.py:265
  51.2 2.0 %collective-permute-start.5 = (f32[4,128,128]{2,1,0:T(8,128)S(1)}, f32[4,128,128]{2,1,0:T(8,128)S(1)}, u32[]{:S(2)}, u32[]{:S(2)}) collective-permute-start(f32[4,128,128]{2,1,0:T(8,128)S(1)} %get-tuple-element.18), channel_id=1, source_target_pairs={{0,8},{8,16},{16,24},{24,32},{32,40},{40,48},{48,56},{56,64},{64,7... | collective-permute-start | bytes 786440 | tf_op jit(solution)/shard_map/ppermute | solution.py:265
  53.2 3.9 %collective-permute-start.6 = (f32[8,128]{1,0:T(8,128)S(1)}, f32[8,128]{1,0:T(8,128)S(1)}, u32[]{:S(2)}, u32[]{:S(2)}) collective-permute-start(f32[8,128]{1,0:T(8,128)S(1)} %get-tuple-element.19), channel_id=1, source_target_pairs={{8,0},{16,8},{24,16},{32,24},{40,32},{48,40},{56,48},{64,56},{72,6... | collective-permute-start | bytes 12296 | tf_op jit(solution)/shard_map/ppermute | solution.py:265
  57.2 4.9 %collective-permute-done.6.left_ref = f32[8,128]{1,0:T(8,128)S(1)} collective-permute-done((f32[8,128]{1,0:T(8,128)S(1)}, f32[8,128]{1,0:T(8,128)S(1)}, u32[]{:S(2)}, u32[]{:S(2)}) %collective-permute-start.6) | collective-permute-done | bytes 4128 | tf_op jit(solution)/shard_map/ppermute | solution.py:265
  62.1 0.0 collective-permute-done.5.side_ref
  62.1 0.0 copy-done.3
  62.1 1.8 %shard_map.114 = (f32[4,128,256]{2,1,0:T(8,128)}, f32[4,128,256]{2,1,0:T(8,128)}, f32[4,128,256]{2,1,0:T(8,128)}) custom-call(f32[4,128,256]{2,1,0:T(8,128)S(1)} %bitcast.12, f32[4,128,256]{2,1,0:T(8,128)S(1)} %bitcast.14, f32[4,128,256]{2,1,0:T(8,128)S(1)} %bitcast.15, f32[4,128,256]{2,1,0:T(8,128)S(1)} %get-tuple-element.13.own_ref, ...), custom_call_target="tpu_custom_call" | custom-call | tf_op jit(solution)/shard_map/pallas_call | solution.py:323
  (11 shorter events, 0.1 us)
Async XLA Ops:
  0.6 3.8 %copy-start = (f32[2,2,128,256]{3,2,1,0:T(8,128)S(1)}, f32[2,2,128,256]{3,2,1,0:T(8,128)}, u32[]{:S(2)}) copy-start(f32[2,2,128,256]{3,2,1,0:T(8,128)} %param.9) | copy-start | bytes 1572868
  1.7 13.3 %collective-permute-start.1 = (f32[4,128,128]{2,1,0:T(8,128)S(1)}, f32[4,128,128]{2,1,0:T(8,128)S(1)}, u32[]{:S(2)}, u32[]{:S(2)}) collective-permute-start(f32[4,128,128]{2,1,0:T(8,128)S(1)} %slice.4), channel_id=1, source_target_pairs={{8,0},{16,8},{24,16},{32,24},{40,32},{48,40},{56,48},{64,56},{72,6... | collective-permute-start | bytes 786440 | tf_op jit(solution)/shard_map/ppermute | solution.py:265
  4.4 16.3 %collective-permute-start = (f32[4,128,256]{2,1,0:T(8,128)S(1)}, f32[4,128,256]{2,1,0:T(8,128)S(1)}, u32[]{:S(2)}, u32[]{:S(2)}) collective-permute-start(f32[4,128,256]{2,1,0:T(8,128)S(1)} %bitcast.10), channel_id=1, source_target_pairs={{1,0},{2,1},{3,2},{4,3},{5,4},{6,5},{7,6},{9,8},{10,9},{11,10},{12... | collective-permute-start | bytes 1572872 | tf_op jit(solution)/shard_map/ppermute | solution.py:265
  14.9 5.8 %collective-permute-start.2 = (f32[4,128,128]{2,1,0:T(8,128)S(1)}, f32[4,128,128]{2,1,0:T(8,128)S(1)}, u32[]{:S(2)}, u32[]{:S(2)}) collective-permute-start(f32[4,128,128]{2,1,0:T(8,128)S(1)} %collective-permute-done.1.right_ref), channel_id=1, source_target_pairs={{1,0},{2,1},{3,2},{4,3},{5,4},{6,5},{7,6},{9,8},{10,9},{11,10},{12... | collective-permute-start | bytes 786440 | tf_op jit(solution)/shard_map/ppermute | solution.py:265
  17.6 3.1 %copy-start.6 = (s32[1,12]{1,0:T(1,128)S(1)}, s32[1,12]{1,0:T(1,128)}, u32[]{:S(2)}) copy-start(s32[1,12]{1,0:T(1,128)} %rows_ref.1) | copy-start | bytes 148
  17.6 3.1 %copy-start.7 = (s32[1,12]{1,0:T(1,128)S(1)}, s32[1,12]{1,0:T(1,128)}, u32[]{:S(2)}) copy-start(s32[1,12]{1,0:T(1,128)} %cols_ref.1) | copy-start | bytes 148
  20.7 1.2 %copy-start.1 = (bf16[4,2,256,256]{3,2,1,0:T(8,128)(2,1)S(1)}, bf16[4,2,256,256]{3,2,1,0:T(8,128)(2,1)}, u32[]{:S(2)}) copy-start(bf16[4,2,256,256]{3,2,1,0:T(8,128)(2,1)} %constant.15.clone.table_ref) | copy-start | bytes 3145732
  22.0 1.1 %copy-start.2 = (f32[1,12,128,128]{3,2,1,0:T(8,128)S(1)}, f32[1,12,128,128]{3,2,1,0:T(8,128)}, u32[]{:S(2)}) copy-start(f32[1,12,128,128]{3,2,1,0:T(8,128)} %param.13) | copy-start | bytes 2359300
  23.1 0.9 %copy-start.5 = (f32[2,128,128]{2,1,0:T(8,128)S(1)}, f32[2,128,128]{2,1,0:T(8,128)}, u32[]{:S(2)}) copy-start(f32[2,128,128]{2,1,0:T(8,128)} %probe_ref.1) | copy-start | bytes 393220
  37.1 14.0 %collective-permute-start.3 = (f32[4,136,384]{2,1,0:T(8,128)S(1)}, f32[4,136,384]{2,1,0:T(8,128)S(1)}, u32[]{:S(2)}, u32[]{:S(2)}) collective-permute-start(f32[4,136,384]{2,1,0:T(8,128)S(1)} %get-tuple-element.14), channel_id=1, source_target_pairs={{0,1},{1,2},{2,3},{3,4},{4,5},{5,6},{6,7},{8,9},{9,10},{10,11},{11... | collective-permute-start | bytes 2506760 | tf_op jit(solution)/shard_map/ppermute | solution.py:265
  39.0 5.2 %collective-permute-start.4 = (f32[8,384]{1,0:T(8,128)S(1)}, f32[8,384]{1,0:T(8,128)S(1)}, u32[]{:S(2)}, u32[]{:S(2)}) collective-permute-start(f32[8,384]{1,0:T(8,128)S(1)} %get-tuple-element.15), channel_id=1, source_target_pairs={{1,0},{2,1},{3,2},{4,3},{5,4},{6,5},{7,6},{9,8},{10,9},{11,10},{12... | collective-permute-start | bytes 36872 | tf_op jit(solution)/shard_map/ppermute | solution.py:265
  51.1 10.9 %copy-start.3 = (f32[2,2,128,256]{3,2,1,0:T(8,128)S(1)}, f32[2,2,128,256]{3,2,1,0:T(8,128)}, u32[]{:S(2)}) copy-start(f32[2,2,128,256]{3,2,1,0:T(8,128)} %param.10) | copy-start | bytes 1572868
  51.1 10.9 %copy-start.4 = (f32[2,2,128,256]{3,2,1,0:T(8,128)S(1)}, f32[2,2,128,256]{3,2,1,0:T(8,128)}, u32[]{:S(2)}) copy-start(f32[2,2,128,256]{3,2,1,0:T(8,128)} %param.11) | copy-start | bytes 1572868
  51.2 10.9 %collective-permute-start.5 = (f32[4,128,128]{2,1,0:T(8,128)S(1)}, f32[4,128,128]{2,1,0:T(8,128)S(1)}, u32[]{:S(2)}, u32[]{:S(2)}) collective-permute-start(f32[4,128,128]{2,1,0:T(8,128)S(1)} %get-tuple-element.18), channel_id=1, source_target_pairs={{0,8},{8,16},{16,24},{24,32},{32,40},{40,48},{48,56},{56,64},{64,7... | collective-permute-start | bytes 786440 | tf_op jit(solution)/shard_map/ppermute | solution.py:265
  53.2 8.8 %collective-permute-start.6 = (f32[8,128]{1,0:T(8,128)S(1)}, f32[8,128]{1,0:T(8,128)S(1)}, u32[]{:S(2)}, u32[]{:S(2)}) collective-permute-start(f32[8,128]{1,0:T(8,128)S(1)} %get-tuple-element.19), channel_id=1, source_target_pairs={{8,0},{16,8},{24,16},{32,24},{40,32},{48,40},{56,48},{64,56},{72,6... | collective-permute-start | bytes 12296 | tf_op jit(solution)/shard_map/ppermute | solution.py:265
where the time goes:
time: 64.2 us; the launch traced here: 63.8 us
  waiting for transfers between devices  24.9 us (39%)
  starting transfers between devices  18.3 us (29%)
  Pallas kernels  14.9 us (23%)
  local copies, waits for them, and re-layouts  4.31 us (7%)
  between operations  1.38 us (2%)
    ppermute x7, waiting for transfers between devices, shift(): return lax.ppermute(block, axis, pairs)  24.9 us
    ppermute x7, starting transfers between devices, shift(): return lax.ppermute(block, axis, pairs)  18.3 us
    pallas_call x1, Pallas kernels, shards(): call(gradient_kernel, [(4, W, 2 * W), (4, W + 8, 3 * W), (8, 3 * W), (4,...  13.1 us
    unnamed x16, local copies, waits for them, and re-layouts  3.28 us
    pallas_call x1, Pallas kernels, shards(): call(update_kernel, [(4, W, 2 * W)] * 3, [VMEM] * 8)  1.78 us
  transfers between devices with their start and end apart: 7, of which 5 were waited for; matrix products, arithmetic and copies ran while one was open for 0% of the time, Pallas kernels for 0%

commit v1 on v0

--- a/solution.py
+++ b/solution.py
@@ -1,4 +1,3 @@
-import functools
 import math
 
 import jax
@@ -19,11 +18,11 @@
 misfit_weight = 1.0 / 64.0
 
 W = 128
-BATCH = 4
 f32 = jnp.float32
 bf16 = jnp.bfloat16
 VMEM = pl.BlockSpec(memory_space=pltpu.VMEM)
 SMEM = pl.BlockSpec(memory_space=pltpu.SMEM)
+HBM = pl.BlockSpec(memory_space=pltpu.HBM)
 
 
 def embedded(matrix):
@@ -90,6 +89,34 @@
     return a[0] * b[0] + a[1] * b[1], a[1] * b[0] - a[0] * b[1]
 
 
+def fetch_kernel(patterns_ref, table_ref, probe_ref, patterns_out, table_out, probe_out, sems):
+    pairs = [
+        (patterns_ref, patterns_out),
+        (table_ref, table_out),
+        (probe_ref, probe_out),
+    ]
+    copies = [pltpu.make_async_copy(a, b, sems.at[i]) for i, (a, b) in enumerate(pairs)]
+    for copy in copies:
+        copy.start()
+    for copy in copies:
+        copy.wait()
+
+
+def smoothed(acc, p, half, t):
+    lane = lax.broadcasted_iota(jnp.int32, (W, W), 1)
+    base = 8 + half * W
+    centre = acc[t, p, base : base + W, :]
+    above = acc[t, p, base - 1 : base - 1 + W, :]
+    under = acc[t, p, base + 1 : base + 1 + W, :]
+    before = pltpu.roll(centre, 1, 1)
+    edge = pltpu.roll(acc[t - 1, p, base : base + W, :], 1, 1) if t else 0.0
+    before = jnp.where(lane == 0, edge, before)
+    after = pltpu.roll(centre, W - 1, 1)
+    edge = pltpu.roll(acc[t + 1, p, base : base + W, :], W - 1, 1) if t < 2 else 0.0
+    after = jnp.where(lane == W - 1, edge, after)
+    return centre + smoothing * (above + under + before + after - 4.0 * centre)
+
+
 def gradient_kernel(
     rows_ref,
     cols_ref,
@@ -99,29 +126,26 @@
     below_ref,
     right_ref,
     corner_ref,
+    corner_too_ref,
     probe_ref,
     patterns_ref,
     table_ref,
-    own_ref,
     down_ref,
     up_ref,
-    side_ref,
-    left_ref,
+    acc,
     obj,
-    acc,
 ):
     for p in range(4):
         for t in range(2):
             obj[t, p, :W, :] = here_ref[p, :, t * W : (t + 1) * W]
             obj[t, p, W:, :] = below_ref[p, :, t * W : (t + 1) * W]
         obj[2, p, :W, :] = right_ref[p]
-        obj[2, p, W:, :] = corner_ref[p]
+        obj[2, p, W:, :] = corner_ref[p] + corner_too_ref[p]
     acc[...] = jnp.zeros_like(acc)
     lane = lax.broadcasted_iota(jnp.int32, (W, W), 1)
     count = count_ref[0, 0]
 
-    def batch(step, carry):
-        slots = [step * BATCH + j for j in range(BATCH)]
+    def batch(slots):
         places = []
         for k in slots:
             col = cols_ref[0, k]
@@ -154,9 +178,14 @@
                 at = pl.ds(row + 8, W)
                 acc[tile, p, at, :] += jnp.where(lane >= shift, turned, 0.0)
                 acc[tile + 1, p, at, :] += jnp.where(lane < shift, turned, 0.0)
-        return carry
-
-    lax.fori_loop(0, (count + BATCH - 1) // BATCH, batch, 0)
+
+    @pl.when(count <= 6)
+    def _():
+        batch(range(6))
+
+    @pl.when(count > 6)
+    def _():
+        batch(range(12))
 
     @pl.when(edge_ref[0, 0] == 1)
     def _():
@@ -166,39 +195,23 @@
     def _():
         acc[:, :, 8 + W :, :] = jnp.zeros((3, 4, acc.shape[2] - 8 - W, W), f32)
 
-    lane = lax.broadcasted_iota(jnp.int32, (W, W), 1)
     down_ref[:, W:, :] = jnp.zeros((4, 8, 3 * W), f32)
     up_ref[...] = jnp.zeros_like(up_ref)
+    for p in range(4):
+        for t in range(3):
+            down_ref[p, :W, t * W : (t + 1) * W] = smoothed(acc, p, 1, t)
+            up_ref[p : p + 1, t * W : (t + 1) * W] = smoothing * acc[t, p, 8:9, :]
+        rim = smoothing * acc[0, p, 8 + W : 8 + 2 * W, :].T[0:1, :]
+        down_ref[p, W : W + 1, :W] = rim
+
+
+def rest_kernel(acc, own_ref, side_ref, left_ref):
     left_ref[...] = jnp.zeros_like(left_ref)
     for p in range(4):
-        for half in range(2):
-            base = 8 + half * W
-            centres = [acc[t, p, base : base + W, :] for t in range(3)]
-            for t in range(3):
-                above = acc[t, p, base - 1 : base - 1 + W, :]
-                under = acc[t, p, base + 1 : base + 1 + W, :]
-                before = pltpu.roll(centres[t], 1, 1)
-                edge = pltpu.roll(centres[t - 1], 1, 1) if t else 0.0
-                before = jnp.where(lane == 0, edge, before)
-                after = pltpu.roll(centres[t], W - 1, 1)
-                edge = pltpu.roll(centres[t + 1], W - 1, 1) if t < 2 else 0.0
-                after = jnp.where(lane == W - 1, edge, after)
-                smooth = centres[t] + smoothing * (
-                    above + under + before + after - 4.0 * centres[t]
-                )
-                if half:
-                    down_ref[p, :W, t * W : (t + 1) * W] = smooth
-                elif t < 2:
-                    own_ref[p, :, t * W : (t + 1) * W] = smooth
-                else:
-                    side_ref[p] = smooth
-            rim = smoothing * centres[0].T[0:1, :]
-            if half:
-                down_ref[p, W : W + 1, :W] = rim
-            else:
-                left_ref[p : p + 1, :] = rim
-        for t in range(3):
-            up_ref[p : p + 1, t * W : (t + 1) * W] = smoothing * acc[t, p, 8:9, :]
+        for t in range(2):
+            own_ref[p, :, t * W : (t + 1) * W] = smoothed(acc, p, 0, t)
+        side_ref[p] = smoothed(acc, p, 0, 2)
+        left_ref[p : p + 1, :] = smoothing * acc[0, p, 8 : 8 + W, :].T[0:1, :]
 
 
 def middle_kernel(side_ref, left_ref, above_ref, under_ref, side_out, left_out):
@@ -235,12 +248,15 @@
     under_ref,
     side_ref,
     left_ref,
-    new_obj,
-    new_first,
-    new_second,
+    obj_out,
+    first_out,
+    second_out,
+    results,
+    sems,
 ):
     row = lax.broadcasted_iota(jnp.int32, (W, W), 0)
     lane = lax.broadcasted_iota(jnp.int32, (W, W), 1)
+    copies = []
     for p in range(4):
         for t in range(2):
             at = (p, slice(None), slice(t * W, (t + 1) * W))
@@ -253,26 +269,38 @@
                 total += jnp.where(lane == W - 1, column, 0.0)
             first = beta_first * first_ref[at] + (1.0 - beta_first) * total
             second = beta_second * second_ref[at] + (1.0 - beta_second) * total * total
-            new_first[at] = first
-            new_second[at] = second
             slope = (first * (1.0 / first_fix)) * lax.rsqrt(second * (1.0 / second_fix))
-            new_obj[at] = obj_ref[at] - rate_scale * arc(slope)
-
-
-def shift(block, axis, distance):
-    count = lax.axis_size(axis)
-    pairs = [(i + distance, i) for i in range(count) if 0 <= i + distance < count]
-    return lax.ppermute(block, axis, pairs)
-
-
-def call(kernel, outs, specs, scratch=()):
+            results[(0,) + at] = obj_ref[at] - rate_scale * arc(slope)
+            results[(1,) + at] = first
+            results[(2,) + at] = second
+        for i, out in enumerate((obj_out, first_out, second_out)):
+            copy = pltpu.make_async_copy(results.at[i, p], out.at[p], sems.at[i, p])
+            copy.start()
+            copies.append(copy)
+    for copy in copies:
+        copy.wait()
+
+
+def permute(block, down, along, takes=None):
+    rows, tiles = lax.axis_size("gy"), lax.axis_size("gx")
+    pairs = []
+    for b in range(tiles):
+        for a in range(rows):
+            there = 0 <= a + down < rows and 0 <= b + along < tiles
+            if there and (takes is None or a % 2 == takes):
+                pairs.append(((b + along) * rows + a + down, b * rows + a))
+    return lax.ppermute(block, ("gx", "gy"), pairs)
+
+
+def call(kernel, outs, ins, scratch=(), space=VMEM, flops=0, nbytes=0):
     return pl.pallas_call(
         kernel,
-        out_shape=[jax.ShapeDtypeStruct(s, f32) for s in outs],
-        in_specs=specs,
-        out_specs=[VMEM] * len(outs),
+        out_shape=[jax.ShapeDtypeStruct(s, d) for s, d in outs],
+        in_specs=ins,
+        out_specs=[space] * len(outs),
         scratch_shapes=scratch,
         compiler_params=pltpu.CompilerParams(vmem_limit_bytes=40 * 1024 * 1024),
+        cost_estimate=pl.CostEstimate(flops=flops, bytes_accessed=nbytes, transcendentals=0),
     )
 
 
@@ -288,20 +316,31 @@
     table,
 ):
     here = object_field.reshape(4, W, 2 * W)
-    right = shift(here[:, :, :W], "gx", 1)
-    below = shift(here, "gy", 1)
-    corner = shift(right, "gy", 1)
+    border = here[:, :, :W]
+    right = permute(border, 0, 1)
+    below = permute(here, 1, 0)
+    corner = permute(border, 1, 1, 1)
+    corner_too = permute(right, 1, 0, 0)
     edge = jnp.stack(
         [
             lax.axis_index("gx") == lax.axis_size("gx") - 1,
             lax.axis_index("gy") == lax.axis_size("gy") - 1,
         ]
     ).astype(jnp.int32)[None]
-    own, down, up, side, left = call(
+    fetched = call(
+        fetch_kernel,
+        [(patterns.shape[1:], f32), (table.shape, bf16), (probe_wave.shape, f32)],
+        [HBM] * 3,
+        [pltpu.SemaphoreType.DMA((3,))],
+        nbytes=4 << 20,
+    )(patterns[0], table, probe_wave)
+    down, up, acc = call(
         gradient_kernel,
-        [(4, W, 2 * W), (4, W + 8, 3 * W), (8, 3 * W), (4, W, W), (8, W)],
-        [SMEM] * 4 + [VMEM] * 7,
-        [pltpu.VMEM((3, 4, 2 * W, W), f32), pltpu.VMEM((3, 4, 2 * W + 16, W), f32)],
+        [((4, W + 8, 3 * W), f32), ((8, 3 * W), f32), ((3, 4, 2 * W + 16, W), f32)],
+        [SMEM] * 4 + [VMEM] * 8,
+        [pltpu.VMEM((3, 4, 2 * W, W), f32)],
+        flops=5 << 30,
+        nbytes=8 << 20,
     )(
         row_offsets,
         col_offsets,
@@ -311,16 +350,34 @@
         below,
         right,
         corner,
-        probe_wave,
-        patterns[0],
-        table,
-    )
-    above = shift(down, "gy", -1)
-    under = shift(up, "gy", 1)
-    side, left = call(middle_kernel, [(4, W, W), (8, W)], [VMEM] * 4)(side, left, above, under)
-    side = shift(side, "gx", -1)
-    left = shift(left, "gx", 1)
-    outs = call(update_kernel, [(4, W, 2 * W)] * 3, [VMEM] * 8)(
+        corner_too,
+        fetched[2],
+        fetched[0],
+        fetched[1],
+    )
+    above = permute(down, -1, 0)
+    under = permute(up, 1, 0)
+    own, side, left = call(
+        rest_kernel,
+        [((4, W, 2 * W), f32), ((4, W, W), f32), ((8, W), f32)],
+        [VMEM],
+        flops=1 << 24,
+        nbytes=2 << 20,
+    )(acc)
+    side, left = call(
+        middle_kernel, [((4, W, W), f32), ((8, W), f32)], [VMEM] * 4, nbytes=1 << 20
+    )(side, left, above, under)
+    side = permute(side, 0, -1)
+    left = permute(left, 0, 1)
+    outs = call(
+        update_kernel,
+        [((4, W, 2 * W), f32)] * 3,
+        [VMEM] * 8,
+        [pltpu.VMEM((3, 4, W, 2 * W), f32), pltpu.SemaphoreType.DMA((3, 4))],
+        HBM,
+        flops=1 << 24,
+        nbytes=4 << 20,
+    )(
         here,
         first_moment.reshape(here.shape),
         second_moment.reshape(here.shape),

time: 64.2 us -> 58.8 us (0.916)
  the two profiles are of different devices: /device:TPU:254 before, /device:TPU:374 now
where the time goes in v1:
time: 58.8 us; the launch traced here: 58.4 us
  starting transfers between devices  19.9 us (34%)
  waiting for transfers between devices  18.6 us (32%)
  Pallas kernels  13.8 us (23%)
  local copies, waits for them, and re-layouts  4.31 us (7%)
  between operations  1.62 us (3%)
    ppermute x8, starting transfers between devices, permute(): return lax.ppermute(block, ('gx', 'gy'), pairs)  19.9 us
    ppermute x8, waiting for transfers between devices, permute(): return lax.ppermute(block, ('gx', 'gy'), pairs)  18.6 us
    pallas_call x1, Pallas kernels, shards(): call(gradient_kernel, [((4, W + 8, 3 * W), f32), ((8, 3 * W), f32), ((3,...  10.8 us
    unnamed x16, local copies, waits for them, and re-layouts  3.28 us
    pallas_call x1, Pallas kernels, shards(): call(update_kernel, [((4, W, 2 * W), f32)] * 3, [VMEM] * 8, [pltpu.VMEM((...  1.81 us
  transfers between devices with their start and end apart: 8, of which 4 were waited for; matrix products, arithmetic and copies ran while one was open for 0% of the time, Pallas kernels for 2%

profile of v1, /device:TPU:374, one launch (start us, length us, event | category | flops | bytes accessed | tf_op | source)
XLA Modules:
  0.0 58.4 jit_solution(17255864385187677613)
XLA Ops:
  0.6 0.0 copy-start
  0.7 1.0 %slice.4 = f32[4,128,128]{2,1,0:T(8,128)S(1)} slice(f32[4,128,256]{2,1,0:T(8,128)} %bitcast.9), slice={[0:4], [0:128], [0:128]} | slice | bytes 524288 | tf_op jit(solution)/shard_map/slice | solution.py:319
  1.7 2.7 %collective-permute-start.1 = (f32[4,128,128]{2,1,0:T(8,128)S(1)}, f32[4,128,128]{2,1,0:T(8,128)S(1)}, u32[]{:S(2)}, u32[]{:S(2)}) collective-permute-start(f32[4,128,128]{2,1,0:T(8,128)S(1)} %slice.4), channel_id=1, source_target_pairs={{8,0},{9,1},{10,2},{11,3},{12,4},{13,5},{14,6},{15,7},{16,8},{17,9... | collective-permute-start | bytes 786440 | tf_op jit(solution)/shard_map/ppermute | solution.py:292
  4.4 1.9 %collective-permute-start = (f32[4,128,256]{2,1,0:T(8,128)}, f32[4,128,256]{2,1,0:T(8,128)S(1)}, u32[]{:S(2)}, u32[]{:S(2)}) collective-permute-start(f32[4,128,256]{2,1,0:T(8,128)} %bitcast.10), channel_id=1, source_target_pairs={{1,0},{2,1},{3,2},{4,3},{5,4},{6,5},{7,6},{9,8},{10,9},{11,10},{12... | collective-permute-start | bytes 1572872 | tf_op jit(solution)/shard_map/ppermute | solution.py:292
  6.4 2.4 %collective-permute-start.2 = (f32[4,128,128]{2,1,0:T(8,128)S(1)}, f32[4,128,128]{2,1,0:T(8,128)S(1)}, u32[]{:S(2)}, u32[]{:S(2)}) collective-permute-start(f32[4,128,128]{2,1,0:T(8,128)S(1)} %slice.4), channel_id=1, source_target_pairs={{10,1},{12,3},{14,5},{18,9},{20,11},{22,13},{26,17},{28,19},{30,21... | collective-permute-start | bytes 786440 | tf_op jit(solution)/shard_map/ppermute | solution.py:292
  8.8 6.1 %collective-permute-done.1.right_ref = f32[4,128,128]{2,1,0:T(8,128)S(1)} collective-permute-done((f32[4,128,128]{2,1,0:T(8,128)S(1)}, f32[4,128,128]{2,1,0:T(8,128)S(1)}, u32[]{:S(2)}, u32[]{:S(2)}) %collective-permute-start.1) | collective-permute-done | bytes 262176 | tf_op jit(solution)/shard_map/ppermute | solution.py:292
  14.9 1.3 %collective-permute-start.3 = (f32[4,128,128]{2,1,0:T(8,128)S(1)}, f32[4,128,128]{2,1,0:T(8,128)S(1)}, u32[]{:S(2)}, u32[]{:S(2)}) collective-permute-start(f32[4,128,128]{2,1,0:T(8,128)S(1)} %collective-permute-done.1.right_ref), channel_id=1, source_target_pairs={{1,0},{3,2},{5,4},{7,6},{9,8},{11,10},{13,12},{15,14},{17,16},{19,... | collective-permute-start | bytes 786440 | tf_op jit(solution)/shard_map/ppermute | solution.py:292
  16.9 0.0 copy-start.1
  16.9 1.2 %copy-done.1 = bf16[4,2,256,256]{3,2,1,0:T(8,128)(2,1)S(1)} copy-done((bf16[4,2,256,256]{3,2,1,0:T(8,128)(2,1)S(1)}, bf16[4,2,256,256]{3,2,1,0:T(8,128)(2,1)}, u32[]{:S(2)}) %copy-start.1) | copy-done | bytes 1048600
  18.1 1.1 %copy-done.2 = f32[1,12,128,128]{3,2,1,0:T(8,128)S(1)} copy-done((f32[1,12,128,128]{3,2,1,0:T(8,128)S(1)}, f32[1,12,128,128]{3,2,1,0:T(8,128)}, u32[]{:S(2)}) %copy-start.2) | copy-done | bytes 786456
  19.3 0.9 %copy-done.5 = f32[2,128,128]{2,1,0:T(8,128)S(1)} copy-done((f32[2,128,128]{2,1,0:T(8,128)S(1)}, f32[2,128,128]{2,1,0:T(8,128)}, u32[]{:S(2)}) %copy-start.5) | copy-done | bytes 131096
  20.2 0.3 shard_map.112
  20.5 0.1 add_convert_fusion.edge_ref
  20.6 10.8 %shard_map.113 = (f32[4,136,384]{2,1,0:T(8,128)S(1)}, f32[8,384]{1,0:T(8,128)S(1)}, f32[3,4,272,128]{3,2,1,0:T(8,128)S(1)}) custom-call(s32[1,12]{1,0:T(1,128)S(1)} %copy-done.6, s32[1,12]{1,0:T(1,128)S(1)} %copy-done.7, s32[1,1]{1,0:T(1,128)S(6)} %copy.12.count_ref, s32[1,2]{1,0:T(1,128)S(1)} %add_convert_fusion.edge_ref, f32[4,128,256]{2,1,0:T(8,128)S(1)} %bitcast.11, ...), custom_call_target="tpu_custom_call" | custom-call | flops 5368709120 | bytes 8388608 | tf_op jit(solution)/shard_map/pallas_call | solution.py:337
  31.4 0.0 copy-start.3
  31.5 2.1 %collective-permute-start.4 = (f32[4,136,384]{2,1,0:T(8,128)S(1)}, f32[4,136,384]{2,1,0:T(8,128)S(1)}, u32[]{:S(2)}, u32[]{:S(2)}) collective-permute-start(f32[4,136,384]{2,1,0:T(8,128)S(1)} %get-tuple-element.22), channel_id=1, source_target_pairs={{0,1},{1,2},{2,3},{3,4},{4,5},{5,6},{6,7},{8,9},{9,10},{10,11},{11... | collective-permute-start | bytes 2506760 | tf_op jit(solution)/shard_map/ppermute | solution.py:292
  33.5 3.6 %collective-permute-start.5 = (f32[8,384]{1,0:T(8,128)S(1)}, f32[8,384]{1,0:T(8,128)S(1)}, u32[]{:S(2)}, u32[]{:S(2)}) collective-permute-start(f32[8,384]{1,0:T(8,128)S(1)} %get-tuple-element.23), channel_id=1, source_target_pairs={{1,0},{2,1},{3,2},{4,3},{5,4},{6,5},{7,6},{9,8},{10,9},{11,10},{12... | collective-permute-start | bytes 36872 | tf_op jit(solution)/shard_map/ppermute | solution.py:292
  37.2 0.9 %shard_map.114 = (f32[4,128,256]{2,1,0:T(8,128)S(1)}, f32[4,128,128]{2,1,0:T(8,128)S(1)}, f32[8,128]{1,0:T(8,128)S(1)}) custom-call(f32[3,4,272,128]{3,2,1,0:T(8,128)S(1)} %get-tuple-element.20.acc), custom_call_target="tpu_custom_call" | custom-call | flops 16777216 | bytes 2097152 | tf_op jit(solution)/shard_map/pallas_call | solution.py:360
  38.0 0.5 collective-permute-done.5.under_ref
  38.5 6.9 %collective-permute-done.4.above_ref = f32[4,136,384]{2,1,0:T(8,128)S(1)} collective-permute-done((f32[4,136,384]{2,1,0:T(8,128)S(1)}, f32[4,136,384]{2,1,0:T(8,128)S(1)}, u32[]{:S(2)}, u32[]{:S(2)}) %collective-permute-start.4) | collective-permute-done | bytes 835616 | tf_op jit(solution)/shard_map/ppermute | solution.py:292
  45.5 2.1 %collective-permute-start.6 = (f32[4,128,128]{2,1,0:T(8,128)S(1)}, f32[4,128,128]{2,1,0:T(8,128)S(1)}, u32[]{:S(2)}, u32[]{:S(2)}) collective-permute-start(f32[4,128,128]{2,1,0:T(8,128)S(1)} %get-tuple-element.26), channel_id=1, source_target_pairs={{0,8},{1,9},{2,10},{3,11},{4,12},{5,13},{6,14},{7,15},{8,16},{9,17... | collective-permute-start | bytes 786440 | tf_op jit(solution)/shard_map/ppermute | solution.py:292
  47.6 3.8 %collective-permute-start.7 = (f32[8,128]{1,0:T(8,128)S(1)}, f32[8,128]{1,0:T(8,128)S(1)}, u32[]{:S(2)}, u32[]{:S(2)}) collective-permute-start(f32[8,128]{1,0:T(8,128)S(1)} %get-tuple-element.27), channel_id=1, source_target_pairs={{8,0},{9,1},{10,2},{11,3},{12,4},{13,5},{14,6},{15,7},{16,8},{17,9... | collective-permute-start | bytes 12296 | tf_op jit(solution)/shard_map/ppermute | solution.py:292
  51.3 5.1 %collective-permute-done.7.left_ref = f32[8,128]{1,0:T(8,128)S(1)} collective-permute-done((f32[8,128]{1,0:T(8,128)S(1)}, f32[8,128]{1,0:T(8,128)S(1)}, u32[]{:S(2)}, u32[]{:S(2)}) %collective-permute-start.7) | collective-permute-done | bytes 4128 | tf_op jit(solution)/shard_map/ppermute | solution.py:292
  56.4 1.8 %shard_map.116 = (f32[4,128,256]{2,1,0:T(8,128)}, f32[4,128,256]{2,1,0:T(8,128)}, f32[4,128,256]{2,1,0:T(8,128)}) custom-call(f32[4,128,256]{2,1,0:T(8,128)S(1)} %bitcast.12, f32[4,128,256]{2,1,0:T(8,128)S(1)} %bitcast.14, f32[4,128,256]{2,1,0:T(8,128)S(1)} %bitcast.15, f32[4,128,256]{2,1,0:T(8,128)S(1)} %get-tuple-element.21.own_ref, ...), custom_call_target="tpu_custom_call" | custom-call | flops 16777216 | bytes 4194304 | tf_op jit(solution)/shard_map/pallas_call | solution.py:372
  (15 shorter events, 0.1 us)
Async XLA Ops:
  0.6 20.0 %copy-start = (f32[2,2,128,256]{3,2,1,0:T(8,128)S(1)}, f32[2,2,128,256]{3,2,1,0:T(8,128)}, u32[]{:S(2)}) copy-start(f32[2,2,128,256]{3,2,1,0:T(8,128)} %param.9) | copy-start | bytes 1572868
  0.6 19.9 %copy-start.7 = (s32[1,12]{1,0:T(1,128)S(1)}, s32[1,12]{1,0:T(1,128)}, u32[]{:S(2)}) copy-start(s32[1,12]{1,0:T(1,128)} %cols_ref.1) | copy-start | bytes 148
  0.7 19.9 %copy-start.6 = (s32[1,12]{1,0:T(1,128)S(1)}, s32[1,12]{1,0:T(1,128)}, u32[]{:S(2)}) copy-start(s32[1,12]{1,0:T(1,128)} %rows_ref.1) | copy-start | bytes 148
  1.7 13.3 %collective-permute-start.1 = (f32[4,128,128]{2,1,0:T(8,128)S(1)}, f32[4,128,128]{2,1,0:T(8,128)S(1)}, u32[]{:S(2)}, u32[]{:S(2)}) collective-permute-start(f32[4,128,128]{2,1,0:T(8,128)S(1)} %slice.4), channel_id=1, source_target_pairs={{8,0},{9,1},{10,2},{11,3},{12,4},{13,5},{14,6},{15,7},{16,8},{17,9... | collective-permute-start | bytes 786440 | tf_op jit(solution)/shard_map/ppermute | solution.py:292
  4.4 16.1 %collective-permute-start = (f32[4,128,256]{2,1,0:T(8,128)}, f32[4,128,256]{2,1,0:T(8,128)S(1)}, u32[]{:S(2)}, u32[]{:S(2)}) collective-permute-start(f32[4,128,256]{2,1,0:T(8,128)} %bitcast.10), channel_id=1, source_target_pairs={{1,0},{2,1},{3,2},{4,3},{5,4},{6,5},{7,6},{9,8},{10,9},{11,10},{12... | collective-permute-start | bytes 1572872 | tf_op jit(solution)/shard_map/ppermute | solution.py:292
  6.4 14.2 %collective-permute-start.2 = (f32[4,128,128]{2,1,0:T(8,128)S(1)}, f32[4,128,128]{2,1,0:T(8,128)S(1)}, u32[]{:S(2)}, u32[]{:S(2)}) collective-permute-start(f32[4,128,128]{2,1,0:T(8,128)S(1)} %slice.4), channel_id=1, source_target_pairs={{10,1},{12,3},{14,5},{18,9},{20,11},{22,13},{26,17},{28,19},{30,21... | collective-permute-start | bytes 786440 | tf_op jit(solution)/shard_map/ppermute | solution.py:292
  14.9 5.6 %collective-permute-start.3 = (f32[4,128,128]{2,1,0:T(8,128)S(1)}, f32[4,128,128]{2,1,0:T(8,128)S(1)}, u32[]{:S(2)}, u32[]{:S(2)}) collective-permute-start(f32[4,128,128]{2,1,0:T(8,128)S(1)} %collective-permute-done.1.right_ref), channel_id=1, source_target_pairs={{1,0},{3,2},{5,4},{7,6},{9,8},{11,10},{13,12},{15,14},{17,16},{19,... | collective-permute-start | bytes 786440 | tf_op jit(solution)/shard_map/ppermute | solution.py:292
  16.9 1.2 %copy-start.1 = (bf16[4,2,256,256]{3,2,1,0:T(8,128)(2,1)S(1)}, bf16[4,2,256,256]{3,2,1,0:T(8,128)(2,1)}, u32[]{:S(2)}) copy-start(bf16[4,2,256,256]{3,2,1,0:T(8,128)(2,1)} %constant.15.clone.table_ref) | copy-start | bytes 3145732
  18.1 1.1 %copy-start.2 = (f32[1,12,128,128]{3,2,1,0:T(8,128)S(1)}, f32[1,12,128,128]{3,2,1,0:T(8,128)}, u32[]{:S(2)}) copy-start(f32[1,12,128,128]{3,2,1,0:T(8,128)} %param.13) | copy-start | bytes 2359300
  19.3 0.9 %copy-start.5 = (f32[2,128,128]{2,1,0:T(8,128)S(1)}, f32[2,128,128]{2,1,0:T(8,128)}, u32[]{:S(2)}) copy-start(f32[2,128,128]{2,1,0:T(8,128)} %probe_ref.1) | copy-start | bytes 393220
  31.4 25.0 %copy-start.3 = (f32[2,2,128,256]{3,2,1,0:T(8,128)S(1)}, f32[2,2,128,256]{3,2,1,0:T(8,128)}, u32[]{:S(2)}) copy-start(f32[2,2,128,256]{3,2,1,0:T(8,128)} %param.10) | copy-start | bytes 1572868
  31.4 24.9 %copy-start.4 = (f32[2,2,128,256]{3,2,1,0:T(8,128)S(1)}, f32[2,2,128,256]{3,2,1,0:T(8,128)}, u32[]{:S(2)}) copy-start(f32[2,2,128,256]{3,2,1,0:T(8,128)} %param.11) | copy-start | bytes 1572868
  31.5 14.0 %collective-permute-start.4 = (f32[4,136,384]{2,1,0:T(8,128)S(1)}, f32[4,136,384]{2,1,0:T(8,128)S(1)}, u32[]{:S(2)}, u32[]{:S(2)}) collective-permute-start(f32[4,136,384]{2,1,0:T(8,128)S(1)} %get-tuple-element.22), channel_id=1, source_target_pairs={{0,1},{1,2},{2,3},{3,4},{4,5},{5,6},{6,7},{8,9},{9,10},{10,11},{11... | collective-permute-start | bytes 2506760 | tf_op jit(solution)/shard_map/ppermute | solution.py:292
  33.5 5.0 %collective-permute-start.5 = (f32[8,384]{1,0:T(8,128)S(1)}, f32[8,384]{1,0:T(8,128)S(1)}, u32[]{:S(2)}, u32[]{:S(2)}) collective-permute-start(f32[8,384]{1,0:T(8,128)S(1)} %get-tuple-element.23), channel_id=1, source_target_pairs={{1,0},{2,1},{3,2},{4,3},{5,4},{6,5},{7,6},{9,8},{10,9},{11,10},{12... | collective-permute-start | bytes 36872 | tf_op jit(solution)/shard_map/ppermute | solution.py:292
  45.5 10.9 %collective-permute-start.6 = (f32[4,128,128]{2,1,0:T(8,128)S(1)}, f32[4,128,128]{2,1,0:T(8,128)S(1)}, u32[]{:S(2)}, u32[]{:S(2)}) collective-permute-start(f32[4,128,128]{2,1,0:T(8,128)S(1)} %get-tuple-element.26), channel_id=1, source_target_pairs={{0,8},{1,9},{2,10},{3,11},{4,12},{5,13},{6,14},{7,15},{8,16},{9,17... | collective-permute-start | bytes 786440 | tf_op jit(solution)/shard_map/ppermute | solution.py:292
  47.6 8.8 %collective-permute-start.7 = (f32[8,128]{1,0:T(8,128)S(1)}, f32[8,128]{1,0:T(8,128)S(1)}, u32[]{:S(2)}, u32[]{:S(2)}) collective-permute-start(f32[8,128]{1,0:T(8,128)S(1)} %get-tuple-element.27), channel_id=1, source_target_pairs={{8,0},{9,1},{10,2},{11,3},{12,4},{13,5},{14,6},{15,7},{16,8},{17,9... | collective-permute-start | bytes 12296 | tf_op jit(solution)/shard_map/ppermute | solution.py:292

commit v2 on v1

--- a/solution.py
+++ b/solution.py
@@ -18,6 +18,8 @@
 misfit_weight = 1.0 / 64.0
 
 W = 128
+SIX = (range(3), range(3, 6))
+TWELVE = (range(6), range(6, 12))
 f32 = jnp.float32
 bf16 = jnp.bfloat16
 VMEM = pl.BlockSpec(memory_space=pltpu.VMEM)
@@ -131,6 +133,7 @@
     patterns_ref,
     table_ref,
     down_ref,
+    across_ref,
     up_ref,
     acc,
     obj,
@@ -145,47 +148,72 @@
     lane = lax.broadcasted_iota(jnp.int32, (W, W), 1)
     count = count_ref[0, 0]
 
-    def batch(slots):
-        places = []
-        for k in slots:
-            col = cols_ref[0, k]
-            places.append((rows_ref[0, k], col // W, col % W))
-        windows = []
-        for row, tile, shift in places:
-            planes = []
-            for p in range(4):
-                first = obj[tile, p, pl.ds(row, W), :]
-                second = obj[tile + 1, p, pl.ds(row, W), :]
-                chosen = jnp.where(lane >= shift, first, second)
-                planes.append(pltpu.roll(chosen, (W - shift) % W, 1))
-            windows.append(((planes[0], planes[2]), (planes[1], planes[3])))
-        probe = (probe_ref[0], probe_ref[1])
-        waves = [times(probe, window[0]) for window in windows]
-        waves = both_sides(waves, table_ref, HOP)
-        fars = both_sides([times(w, o[1]) for w, o in zip(waves, windows)], table_ref, DFT)
-        back = []
-        for k, far in zip(slots, fars):
-            misfit = far[0] * far[0] + far[1] * far[1] - patterns_ref[k]
+    probe = (probe_ref[0], probe_ref[1])
+
+    def place(k):
+        col = cols_ref[0, k]
+        return rows_ref[0, k], col // W, col % W
+
+    def window(k, s):
+        row, tile, shift = place(k)
+        planes = []
+        for p in (s, 2 + s):
+            first = obj[tile, p, pl.ds(row, W), :]
+            second = obj[tile + 1, p, pl.ds(row, W), :]
+            chosen = jnp.where(lane >= shift, first, second)
+            planes.append(pltpu.roll(chosen, (W - shift) % W, 1))
+        return tuple(planes)
+
+    def scatter(k, s, plane_pair):
+        row, tile, shift = place(k)
+        at = pl.ds(row + 8, W)
+        for p, plane in zip((s, 2 + s), plane_pair):
+            turned = pltpu.roll(plane, shift, 1)
+            acc[tile, p, at, :] += jnp.where(lane >= shift, turned, 0.0)
+            acc[tile + 1, p, at, :] += jnp.where(lane < shift, turned, 0.0)
+
+    def hop(state):
+        waves = [times(probe, window(k, 0)) for k in state["slots"]]
+        state["waves"] = both_sides(waves, table_ref, HOP)
+
+    def far(state):
+        state["object"] = [window(k, 1) for k in state["slots"]]
+        waves = [times(w, o) for w, o in zip(state["waves"], state["object"])]
+        state["far"] = both_sides(waves, table_ref, DFT)
+
+    def back(state):
+        grads = []
+        for k, wave in zip(state["slots"], state["far"]):
+            misfit = wave[0] * wave[0] + wave[1] * wave[1] - patterns_ref[k]
             misfit = misfit * jnp.where(k < count, 4.0 * misfit_weight, 0.0)
-            back.append((misfit * far[0], misfit * far[1]))
-        back = both_sides(back, table_ref, DFT_CONJ)
-        second = [times_conj(g, w) for g, w in zip(back, waves)]
-        back = both_sides([times_conj(g, o[1]) for g, o in zip(back, windows)], table_ref, HOP_CONJ)
-        first = [times_conj(g, probe) for g in back]
-        for (row, tile, shift), one, two in zip(places, first, second):
-            for p, plane in enumerate((one[0], two[0], one[1], two[1])):
-                turned = pltpu.roll(plane, shift, 1)
-                at = pl.ds(row + 8, W)
-                acc[tile, p, at, :] += jnp.where(lane >= shift, turned, 0.0)
-                acc[tile + 1, p, at, :] += jnp.where(lane < shift, turned, 0.0)
+            grads.append((misfit * wave[0], misfit * wave[1]))
+        state["back"] = both_sides(grads, table_ref, DFT_CONJ)
+
+    def hop_back(state):
+        for k, g, w in zip(state["slots"], state["back"], state["waves"]):
+            scatter(k, 1, times_conj(g, w))
+        grads = [times_conj(g, o) for g, o in zip(state["back"], state["object"])]
+        state["first"] = both_sides(grads, table_ref, HOP_CONJ)
+
+    def finish(state):
+        for k, g in zip(state["slots"], state["first"]):
+            scatter(k, 0, times_conj(g, probe))
+
+    def batch(groups):
+        stages = (hop, far, back, hop_back, finish)
+        states = [{"slots": slots} for slots in groups]
+        for turn in range(len(stages) + len(states) - 1):
+            for i, state in enumerate(states):
+                if 0 <= turn - i < len(stages):
+                    stages[turn - i](state)
 
     @pl.when(count <= 6)
     def _():
-        batch(range(6))
+        batch(SIX)
 
     @pl.when(count > 6)
     def _():
-        batch(range(12))
+        batch(TWELVE)
 
     @pl.when(edge_ref[0, 0] == 1)
     def _():
@@ -195,14 +223,16 @@
     def _():
         acc[:, :, 8 + W :, :] = jnp.zeros((3, 4, acc.shape[2] - 8 - W, W), f32)
 
-    down_ref[:, W:, :] = jnp.zeros((4, 8, 3 * W), f32)
+    across_ref[:, W:, :] = jnp.zeros((4, 8, W), f32)
     up_ref[...] = jnp.zeros_like(up_ref)
     for p in range(4):
+        for t in range(2):
+            down_ref[p, :, t * W : (t + 1) * W] = smoothed(acc, p, 1, t)
+        across_ref[p, :W, :] = smoothed(acc, p, 1, 2)
+        rim = smoothing * acc[0, p, 8 + W : 8 + 2 * W, :].T[0:1, :]
+        across_ref[p, W : W + 1, :] = rim
         for t in range(3):
-            down_ref[p, :W, t * W : (t + 1) * W] = smoothed(acc, p, 1, t)
             up_ref[p : p + 1, t * W : (t + 1) * W] = smoothing * acc[t, p, 8:9, :]
-        rim = smoothing * acc[0, p, 8 + W : 8 + 2 * W, :].T[0:1, :]
-        down_ref[p, W : W + 1, :W] = rim
 
 
 def rest_kernel(acc, own_ref, side_ref, left_ref):
@@ -214,13 +244,13 @@
         left_ref[p : p + 1, :] = smoothing * acc[0, p, 8 : 8 + W, :].T[0:1, :]
 
 
-def middle_kernel(side_ref, left_ref, above_ref, under_ref, side_out, left_out):
-    for p in range(4):
-        side_out[p] = side_ref[p] + above_ref[p, :W, 2 * W :]
+def middle_kernel(side_ref, left_ref, across_ref, under_ref, side_out, left_out):
+    for p in range(4):
+        side_out[p] = side_ref[p] + across_ref[p, :W, :]
         side_out[p, W - 1 : W, :] += under_ref[p : p + 1, 2 * W :]
     left_out[...] = left_ref[...]
     for p in range(4):
-        left_out[p : p + 1, :] += above_ref[p, W : W + 1, :W]
+        left_out[p : p + 1, :] += across_ref[p, W : W + 1, :]
 
 
 def arc(slope):
@@ -239,44 +269,50 @@
     return jnp.where(slope < 0.0, -value, value)
 
 
-def update_kernel(
-    obj_ref,
-    first_ref,
-    second_ref,
-    own_ref,
-    above_ref,
-    under_ref,
-    side_ref,
-    left_ref,
-    obj_out,
-    first_out,
-    second_out,
-    results,
-    sems,
+def updated(t, refs, total, results, outs, sems, p):
+    at = (p, slice(None), slice(t * W, (t + 1) * W))
+    obj_ref, first_ref, second_ref = refs
+    first = beta_first * first_ref[at] + (1.0 - beta_first) * total
+    second = beta_second * second_ref[at] + (1.0 - beta_second) * total * total
+    slope = (first * (1.0 / first_fix)) * lax.rsqrt(second * (1.0 / second_fix))
+    results[0, p] = obj_ref[at] - rate_scale * arc(slope)
+    results[1, p] = first
+    results[2, p] = second
+    copies = []
+    for i, out in enumerate(outs):
+        copy = pltpu.make_async_copy(results.at[i, p], out.at[at], sems.at[i, p])
+        copy.start()
+        copies.append(copy)
+    return copies
+
+
+def right_update_kernel(
+    obj_ref, first_ref, second_ref, own_ref, above_ref, under_ref, left_ref, *outs_and_scratch
 ):
+    *outs, results, sems = outs_and_scratch
     row = lax.broadcasted_iota(jnp.int32, (W, W), 0)
     lane = lax.broadcasted_iota(jnp.int32, (W, W), 1)
     copies = []
     for p in range(4):
-        for t in range(2):
-            at = (p, slice(None), slice(t * W, (t + 1) * W))
-            total = own_ref[at] + above_ref[p, :W, t * W : (t + 1) * W]
-            total += jnp.where(row == W - 1, under_ref[p : p + 1, t * W : (t + 1) * W], 0.0)
-            if t == 0:
-                total += side_ref[p]
-            else:
-                column = jnp.broadcast_to(left_ref[p : p + 1, :], (W, W)).T
-                total += jnp.where(lane == W - 1, column, 0.0)
-            first = beta_first * first_ref[at] + (1.0 - beta_first) * total
-            second = beta_second * second_ref[at] + (1.0 - beta_second) * total * total
-            slope = (first * (1.0 / first_fix)) * lax.rsqrt(second * (1.0 / second_fix))
-            results[(0,) + at] = obj_ref[at] - rate_scale * arc(slope)
-            results[(1,) + at] = first
-            results[(2,) + at] = second
-        for i, out in enumerate((obj_out, first_out, second_out)):
-            copy = pltpu.make_async_copy(results.at[i, p], out.at[p], sems.at[i, p])
-            copy.start()
-            copies.append(copy)
+        total = own_ref[p, :, W:] + above_ref[p, :, W:]
+        total += jnp.where(row == W - 1, under_ref[p : p + 1, W : 2 * W], 0.0)
+        column = jnp.broadcast_to(left_ref[p : p + 1, :], (W, W)).T
+        total += jnp.where(lane == W - 1, column, 0.0)
+        copies += updated(1, (obj_ref, first_ref, second_ref), total, results, outs, sems, p)
+    for copy in copies:
+        copy.wait()
+
+
+def left_update_kernel(
+    obj_ref, first_ref, second_ref, own_ref, above_ref, under_ref, side_ref, *outs_and_scratch
+):
+    *outs, results, sems = outs_and_scratch[3:]
+    row = lax.broadcasted_iota(jnp.int32, (W, W), 0)
+    copies = []
+    for p in range(4):
+        total = own_ref[p, :, :W] + above_ref[p, :, :W] + side_ref[p]
+        total += jnp.where(row == W - 1, under_ref[p : p + 1, :W], 0.0)
+        copies += updated(0, (obj_ref, first_ref, second_ref), total, results, outs, sems, p)
     for copy in copies:
         copy.wait()
 
@@ -292,13 +328,14 @@
     return lax.ppermute(block, ("gx", "gy"), pairs)
 
 
-def call(kernel, outs, ins, scratch=(), space=VMEM, flops=0, nbytes=0):
+def call(kernel, outs, ins, scratch=(), space=VMEM, flops=0, nbytes=0, aliases=None):
     return pl.pallas_call(
         kernel,
         out_shape=[jax.ShapeDtypeStruct(s, d) for s, d in outs],
         in_specs=ins,
         out_specs=[space] * len(outs),
         scratch_shapes=scratch,
+        input_output_aliases=aliases or {},
         compiler_params=pltpu.CompilerParams(vmem_limit_bytes=40 * 1024 * 1024),
         cost_estimate=pl.CostEstimate(flops=flops, bytes_accessed=nbytes, transcendentals=0),
     )
@@ -333,10 +370,15 @@
         [HBM] * 3,
         [pltpu.SemaphoreType.DMA((3,))],
         nbytes=4 << 20,
-    )(patterns[0], table, probe_wave)
-    down, up, acc = call(
+    )(*(pltpu.with_memory_space_constraint(x, pltpu.HBM) for x in (patterns[0], table, probe_wave)))
+    down, across, up, acc = call(
         gradient_kernel,
-        [((4, W + 8, 3 * W), f32), ((8, 3 * W), f32), ((3, 4, 2 * W + 16, W), f32)],
+        [
+            ((4, W, 2 * W), f32),
+            ((4, W + 8, W), f32),
+            ((8, 3 * W), f32),
+            ((3, 4, 2 * W + 16, W), f32),
+        ],
         [SMEM] * 4 + [VMEM] * 8,
         [pltpu.VMEM((3, 4, 2 * W, W), f32)],
         flops=5 << 30,
@@ -355,6 +397,7 @@
         fetched[0],
         fetched[1],
     )
+    across = permute(across, -1, 0)
     above = permute(down, -1, 0)
     under = permute(up, 1, 0)
     own, side, left = call(
@@ -366,27 +409,25 @@
     )(acc)
     side, left = call(
         middle_kernel, [((4, W, W), f32), ((8, W), f32)], [VMEM] * 4, nbytes=1 << 20
-    )(side, left, above, under)
+    )(side, left, across, under)
+    left = permute(left, 0, 1)
     side = permute(side, 0, -1)
-    left = permute(left, 0, 1)
+    moments = first_moment.reshape(here.shape), second_moment.reshape(here.shape)
+    scratch = [pltpu.VMEM((3, 4, W, W), f32), pltpu.SemaphoreType.DMA((3, 4))]
+    whole = [((4, W, 2 * W), f32)] * 3
     outs = call(
-        update_kernel,
-        [((4, W, 2 * W), f32)] * 3,
-        [VMEM] * 8,
-        [pltpu.VMEM((3, 4, W, 2 * W), f32), pltpu.SemaphoreType.DMA((3, 4))],
+        right_update_kernel, whole, [VMEM] * 7, scratch, HBM, flops=1 << 24, nbytes=2 << 20
+    )(here, *moments, own, above, under, left)
+    outs = call(
+        left_update_kernel,
+        whole,
+        [VMEM] * 7 + [HBM] * 3,
+        scratch,
         HBM,
         flops=1 << 24,
-        nbytes=4 << 20,
-    )(
-        here,
-        first_moment.reshape(here.shape),
-        second_moment.reshape(here.shape),
-        own,
-        above,
-        under,
-        side,
-        left,
-    )
+        nbytes=2 << 20,
+        aliases={7: 0, 8: 1, 9: 2},
+    )(here, *moments, own, above, under, side, *outs)
     return tuple(out.reshape(object_field.shape) for out in outs)
 
 

time: 58.8 us -> 55 us (0.935)
  the two profiles are of different devices: /device:TPU:374 before, /device:TPU:393 now
where the time goes in v2:
time: 55 us; the launch traced here: 55.1 us
  starting transfers between devices  29.5 us (54%)
  Pallas kernels  13.8 us (25%)
  waiting for transfers between devices  9.23 us (17%)
  between operations  1.44 us (3%)
  local copies, waits for them, and re-layouts  1.05 us (2%)
    ppermute x9, starting transfers between devices, permute(): return lax.ppermute(block, ('gx', 'gy'), pairs)  29.5 us
    ppermute x9, waiting for transfers between devices, permute(): return lax.ppermute(block, ('gx', 'gy'), pairs)  9.23 us
    pallas_call x1, Pallas kernels, shards(): call(gradient_kernel, [((4, W, 2 * W), f32), ((4, W + 8, W), f32), ((8, 3...  8.92 us
    pallas_call x1, Pallas kernels, shards(): call(fetch_kernel, [(patterns.shape[1:], f32), (table.shape, bf16), (prob...  1.5 us
    pallas_call x1, Pallas kernels, shards(): call(right_update_kernel, whole, [VMEM] * 7, scratch, HBM, flops=1 << 24,...  1.3 us
    pallas_call x1, Pallas kernels, shards(): call(left_update_kernel, whole, [VMEM] * 7 + [HBM] * 3, scratch, HBM, flo...  1.16 us
  transfers between devices with their start and end apart: 9, of which 6 were waited for; matrix products, arithmetic and copies ran while one was open for 0% of the time, Pallas kernels for 7%

profile of v2, /device:TPU:393, one launch (start us, length us, event | category | flops | bytes accessed | tf_op | source)
XLA Modules:
  0.0 55.1 jit_solution(16572629836949264896)
XLA Ops:
  0.6 0.0 copy-start
  0.7 1.0 %slice.4 = f32[4,128,128]{2,1,0:T(8,128)S(1)} slice(f32[4,128,256]{2,1,0:T(8,128)} %bitcast.9), slice={[0:4], [0:128], [0:128]} | slice | bytes 524288 | tf_op jit(solution)/shard_map/slice | solution.py:356
  1.7 6.0 %collective-permute-start.1 = (f32[4,128,128]{2,1,0:T(8,128)S(1)}, f32[4,128,128]{2,1,0:T(8,128)S(1)}, u32[]{:S(2)}, u32[]{:S(2)}) collective-permute-start(f32[4,128,128]{2,1,0:T(8,128)S(1)} %slice.4), channel_id=1, source_target_pairs={{8,0},{9,1},{10,2},{11,3},{12,4},{13,5},{14,6},{15,7},{16,8},{17,9... | collective-permute-start | bytes 786440 | tf_op jit(solution)/shard_map/ppermute | solution.py:328
  7.7 2.9 %collective-permute-start = (f32[4,128,256]{2,1,0:T(8,128)}, f32[4,128,256]{2,1,0:T(8,128)S(1)}, u32[]{:S(2)}, u32[]{:S(2)}) collective-permute-start(f32[4,128,256]{2,1,0:T(8,128)} %bitcast.10), channel_id=1, source_target_pairs={{1,0},{2,1},{3,2},{4,3},{5,4},{6,5},{7,6},{9,8},{10,9},{11,10},{12... | collective-permute-start | bytes 1572872 | tf_op jit(solution)/shard_map/ppermute | solution.py:328
  10.6 1.3 %collective-permute-start.2 = (f32[4,128,128]{2,1,0:T(8,128)S(1)}, f32[4,128,128]{2,1,0:T(8,128)S(1)}, u32[]{:S(2)}, u32[]{:S(2)}) collective-permute-start(f32[4,128,128]{2,1,0:T(8,128)S(1)} %slice.4), channel_id=1, source_target_pairs={{10,1},{12,3},{14,5},{18,9},{20,11},{22,13},{26,17},{28,19},{30,21... | collective-permute-start | bytes 786440 | tf_op jit(solution)/shard_map/ppermute | solution.py:328
  11.9 0.8 %collective-permute-done.1.right_ref = f32[4,128,128]{2,1,0:T(8,128)S(1)} collective-permute-done((f32[4,128,128]{2,1,0:T(8,128)S(1)}, f32[4,128,128]{2,1,0:T(8,128)S(1)}, u32[]{:S(2)}, u32[]{:S(2)}) %collective-permute-start.1) | collective-permute-done | bytes 262176 | tf_op jit(solution)/shard_map/ppermute | solution.py:328
  12.7 3.5 %collective-permute-start.3 = (f32[4,128,128]{2,1,0:T(8,128)S(1)}, f32[4,128,128]{2,1,0:T(8,128)S(1)}, u32[]{:S(2)}, u32[]{:S(2)}) collective-permute-start(f32[4,128,128]{2,1,0:T(8,128)S(1)} %collective-permute-done.1.right_ref), channel_id=1, source_target_pairs={{1,0},{3,2},{5,4},{7,6},{9,8},{11,10},{13,12},{15,14},{17,16},{19,... | collective-permute-start | bytes 786440 | tf_op jit(solution)/shard_map/ppermute | solution.py:328
  16.8 1.5 %shard_map.112 = (f32[12,128,128]{2,1,0:T(8,128)S(1)}, bf16[4,2,256,256]{3,2,1,0:T(8,128)(2,1)S(1)}, f32[2,128,128]{2,1,0:T(8,128)S(1)}) custom-call(f32[12,128,128]{2,1,0:T(8,128)} %bitcast.18, bf16[4,2,256,256]{3,2,1,0:T(8,128)(2,1)} %constant.15.clone.table_ref, f32[2,128,128]{2,1,0:T(8,128)} %probe_ref.1), custom_call_target="tpu_custom_call" | custom-call | bytes 4194304 | tf_op jit(solution)/shard_map/pallas_call | solution.py:367
  18.3 0.1 add_convert_fusion.edge_ref
  18.4 0.9 %collective-permute-done.2.corner_ref = f32[4,128,128]{2,1,0:T(8,128)S(1)} collective-permute-done((f32[4,128,128]{2,1,0:T(8,128)S(1)}, f32[4,128,128]{2,1,0:T(8,128)S(1)}, u32[]{:S(2)}, u32[]{:S(2)}) %collective-permute-start.2) | collective-permute-done | bytes 262176 | tf_op jit(solution)/shard_map/ppermute | solution.py:328
  19.3 2.4 %collective-permute-done.below_ref = f32[4,128,256]{2,1,0:T(8,128)S(1)} collective-permute-done((f32[4,128,256]{2,1,0:T(8,128)}, f32[4,128,256]{2,1,0:T(8,128)S(1)}, u32[]{:S(2)}, u32[]{:S(2)}) %collective-permute-start) | collective-permute-done | bytes 524320 | tf_op jit(solution)/shard_map/ppermute | solution.py:328
  21.7 8.9 %shard_map.113 = (f32[4,128,256]{2,1,0:T(8,128)S(1)}, f32[4,136,128]{2,1,0:T(8,128)S(1)}, f32[8,384]{1,0:T(8,128)S(1)}, f32[3,4,272,128]{3,2,1,0:T(8,128)S(1)}) custom-call(s32[1,12]{1,0:T(1,128)S(1)} %copy-done.3, s32[1,12]{1,0:T(1,128)S(1)} %copy-done.4, s32[1,1]{1,0:T(1,128)S(6)} %copy.18.count_ref, s32[1,2]{1,0:T(1,128)S(1)} %add_convert_fusion.edge_ref, ...), custom_call_target="tpu_custom_call" | custom-call | flops 5368709120 | bytes 8388608 | tf_op jit(solution)/shard_map/pallas_call | solution.py:374
  30.6 0.0 copy-start.2
  30.6 2.1 %collective-permute-start.6 = (f32[4,136,128]{2,1,0:T(8,128)S(1)}, f32[4,136,128]{2,1,0:T(8,128)S(1)}, u32[]{:S(2)}, u32[]{:S(2)}) collective-permute-start(f32[4,136,128]{2,1,0:T(8,128)S(1)} %get-tuple-element.30), channel_id=1, source_target_pairs={{0,1},{1,2},{2,3},{3,4},{4,5},{5,6},{6,7},{8,9},{9,10},{10,11},{11... | collective-permute-start | bytes 835592 | tf_op jit(solution)/shard_map/ppermute | solution.py:328
  32.7 3.3 %collective-permute-start.4 = (f32[4,128,256]{2,1,0:T(8,128)S(1)}, f32[4,128,256]{2,1,0:T(8,128)S(1)}, u32[]{:S(2)}, u32[]{:S(2)}) collective-permute-start(f32[4,128,256]{2,1,0:T(8,128)S(1)} %get-tuple-element.26), channel_id=1, source_target_pairs={{0,1},{1,2},{2,3},{3,4},{4,5},{5,6},{6,7},{8,9},{9,10},{10,11},{11... | collective-permute-start | bytes 1572872 | tf_op jit(solution)/shard_map/ppermute | solution.py:328
  35.9 1.9 %collective-permute-start.5 = (f32[8,384]{1,0:T(8,128)S(1)}, f32[8,384]{1,0:T(8,128)S(1)}, u32[]{:S(2)}, u32[]{:S(2)}) collective-permute-start(f32[8,384]{1,0:T(8,128)S(1)} %get-tuple-element.27), channel_id=1, source_target_pairs={{1,0},{2,1},{3,2},{4,3},{5,4},{6,5},{7,6},{9,8},{10,9},{11,10},{12... | collective-permute-start | bytes 36872 | tf_op jit(solution)/shard_map/ppermute | solution.py:328
  37.9 0.9 %shard_map.114 = (f32[4,128,256]{2,1,0:T(8,128)S(1)}, f32[4,128,128]{2,1,0:T(8,128)S(1)}, f32[8,128]{1,0:T(8,128)S(1)}) custom-call(f32[3,4,272,128]{3,2,1,0:T(8,128)S(1)} %get-tuple-element.24.acc), custom_call_target="tpu_custom_call" | custom-call | flops 16777216 | bytes 2097152 | tf_op jit(solution)/shard_map/pallas_call | solution.py:403
  38.7 2.5 %collective-permute-done.5.under_ref = f32[8,384]{1,0:T(8,128)S(1)} collective-permute-done((f32[8,384]{1,0:T(8,128)S(1)}, f32[8,384]{1,0:T(8,128)S(1)}, u32[]{:S(2)}, u32[]{:S(2)}) %collective-permute-start.5) | collective-permute-done | bytes 12320 | tf_op jit(solution)/shard_map/ppermute | solution.py:328
  41.3 1.9 %collective-permute-start.7 = (f32[4,128,128]{2,1,0:T(8,128)S(1)}, f32[4,128,128]{2,1,0:T(8,128)S(1)}, u32[]{:S(2)}, u32[]{:S(2)}) collective-permute-start(f32[4,128,128]{2,1,0:T(8,128)S(1)} %get-tuple-element.31), channel_id=1, source_target_pairs={{0,8},{1,9},{2,10},{3,11},{4,12},{5,13},{6,14},{7,15},{8,16},{9,17... | collective-permute-start | bytes 786440 | tf_op jit(solution)/shard_map/ppermute | solution.py:328
  43.2 6.7 %collective-permute-start.8 = (f32[8,128]{1,0:T(8,128)S(1)}, f32[8,128]{1,0:T(8,128)S(1)}, u32[]{:S(2)}, u32[]{:S(2)}) collective-permute-start(f32[8,128]{1,0:T(8,128)S(1)} %get-tuple-element.32), channel_id=1, source_target_pairs={{8,0},{9,1},{10,2},{11,3},{12,4},{13,5},{14,6},{15,7},{16,8},{17,9... | collective-permute-start | bytes 12296 | tf_op jit(solution)/shard_map/ppermute | solution.py:328
  49.9 0.7 %collective-permute-done.8.left_ref = f32[8,128]{1,0:T(8,128)S(1)} collective-permute-done((f32[8,128]{1,0:T(8,128)S(1)}, f32[8,128]{1,0:T(8,128)S(1)}, u32[]{:S(2)}, u32[]{:S(2)}) %collective-permute-start.8) | collective-permute-done | bytes 4128 | tf_op jit(solution)/shard_map/ppermute | solution.py:328
  50.7 1.3 %shard_map.116 = (f32[4,128,256]{2,1,0:T(8,128)}, f32[4,128,256]{2,1,0:T(8,128)}, f32[4,128,256]{2,1,0:T(8,128)}) custom-call(f32[4,128,256]{2,1,0:T(8,128)S(1)} %bitcast.12, f32[4,128,256]{2,1,0:T(8,128)S(1)} %bitcast.14, f32[4,128,256]{2,1,0:T(8,128)S(1)} %bitcast.16, f32[4,128,256]{2,1,0:T(8,128)S(1)} %get-tuple-element.25.own_ref, ...), custom_call_target="tpu_custom_call" | custom-call | flops 16777216 | bytes 2097152 | tf_op jit(solution)/shard_map/pallas_call | solution.py:418
  52.0 1.9 %collective-permute-done.7.side_ref = f32[4,128,128]{2,1,0:T(8,128)S(1)} collective-permute-done((f32[4,128,128]{2,1,0:T(8,128)S(1)}, f32[4,128,128]{2,1,0:T(8,128)S(1)}, u32[]{:S(2)}, u32[]{:S(2)}) %collective-permute-start.7) | collective-permute-done | bytes 262176 | tf_op jit(solution)/shard_map/ppermute | solution.py:328
  53.9 1.2 %shard_map.117 = (f32[4,128,256]{2,1,0:T(8,128)}, f32[4,128,256]{2,1,0:T(8,128)}, f32[4,128,256]{2,1,0:T(8,128)}) custom-call(f32[4,128,256]{2,1,0:T(8,128)S(1)} %bitcast.13, f32[4,128,256]{2,1,0:T(8,128)S(1)} %bitcast.15, f32[4,128,256]{2,1,0:T(8,128)S(1)} %bitcast.17, ...), custom_call_target="tpu_custom_call", output_to_operand_aliasing={{0}: (7, {}), {1}: (8, {}), {2}: (9, {})} | custom-call | flops 16777216 | bytes 2097152 | tf_op jit(solution)/shard_map/pallas_call | solution.py:421
  (12 shorter events, 0.1 us)
Async XLA Ops:
  0.6 21.0 %copy-start = (f32[2,2,128,256]{3,2,1,0:T(8,128)S(1)}, f32[2,2,128,256]{3,2,1,0:T(8,128)}, u32[]{:S(2)}) copy-start(f32[2,2,128,256]{3,2,1,0:T(8,128)} %param.9) | copy-start | bytes 1572868
  0.6 21.0 %copy-start.4 = (s32[1,12]{1,0:T(1,128)S(1)}, s32[1,12]{1,0:T(1,128)}, u32[]{:S(2)}) copy-start(s32[1,12]{1,0:T(1,128)} %cols_ref.1) | copy-start | bytes 148
  0.7 21.0 %copy-start.3 = (s32[1,12]{1,0:T(1,128)S(1)}, s32[1,12]{1,0:T(1,128)}, u32[]{:S(2)}) copy-start(s32[1,12]{1,0:T(1,128)} %rows_ref.1) | copy-start | bytes 148
  1.7 11.0 %collective-permute-start.1 = (f32[4,128,128]{2,1,0:T(8,128)S(1)}, f32[4,128,128]{2,1,0:T(8,128)S(1)}, u32[]{:S(2)}, u32[]{:S(2)}) collective-permute-start(f32[4,128,128]{2,1,0:T(8,128)S(1)} %slice.4), channel_id=1, source_target_pairs={{8,0},{9,1},{10,2},{11,3},{12,4},{13,5},{14,6},{15,7},{16,8},{17,9... | collective-permute-start | bytes 786440 | tf_op jit(solution)/shard_map/ppermute | solution.py:328
  7.7 13.9 %collective-permute-start = (f32[4,128,256]{2,1,0:T(8,128)}, f32[4,128,256]{2,1,0:T(8,128)S(1)}, u32[]{:S(2)}, u32[]{:S(2)}) collective-permute-start(f32[4,128,256]{2,1,0:T(8,128)} %bitcast.10), channel_id=1, source_target_pairs={{1,0},{2,1},{3,2},{4,3},{5,4},{6,5},{7,6},{9,8},{10,9},{11,10},{12... | collective-permute-start | bytes 1572872 | tf_op jit(solution)/shard_map/ppermute | solution.py:328
  10.6 8.7 %collective-permute-start.2 = (f32[4,128,128]{2,1,0:T(8,128)S(1)}, f32[4,128,128]{2,1,0:T(8,128)S(1)}, u32[]{:S(2)}, u32[]{:S(2)}) collective-permute-start(f32[4,128,128]{2,1,0:T(8,128)S(1)} %slice.4), channel_id=1, source_target_pairs={{10,1},{12,3},{14,5},{18,9},{20,11},{22,13},{26,17},{28,19},{30,21... | collective-permute-start | bytes 786440 | tf_op jit(solution)/shard_map/ppermute | solution.py:328
  12.7 6.6 %collective-permute-start.3 = (f32[4,128,128]{2,1,0:T(8,128)S(1)}, f32[4,128,128]{2,1,0:T(8,128)S(1)}, u32[]{:S(2)}, u32[]{:S(2)}) collective-permute-start(f32[4,128,128]{2,1,0:T(8,128)S(1)} %collective-permute-done.1.right_ref), channel_id=1, source_target_pairs={{1,0},{3,2},{5,4},{7,6},{9,8},{11,10},{13,12},{15,14},{17,16},{19,... | collective-permute-start | bytes 786440 | tf_op jit(solution)/shard_map/ppermute | solution.py:328
  30.6 20.1 %copy-start.1 = (f32[2,2,128,256]{3,2,1,0:T(8,128)S(1)}, f32[2,2,128,256]{3,2,1,0:T(8,128)}, u32[]{:S(2)}) copy-start(f32[2,2,128,256]{3,2,1,0:T(8,128)} %param.10) | copy-start | bytes 1572868
  30.6 20.1 %copy-start.2 = (f32[2,2,128,256]{3,2,1,0:T(8,128)S(1)}, f32[2,2,128,256]{3,2,1,0:T(8,128)}, u32[]{:S(2)}) copy-start(f32[2,2,128,256]{3,2,1,0:T(8,128)} %param.11) | copy-start | bytes 1572868
  30.6 10.6 %collective-permute-start.6 = (f32[4,136,128]{2,1,0:T(8,128)S(1)}, f32[4,136,128]{2,1,0:T(8,128)S(1)}, u32[]{:S(2)}, u32[]{:S(2)}) collective-permute-start(f32[4,136,128]{2,1,0:T(8,128)S(1)} %get-tuple-element.30), channel_id=1, source_target_pairs={{0,1},{1,2},{2,3},{3,4},{4,5},{5,6},{6,7},{8,9},{9,10},{10,11},{11... | collective-permute-start | bytes 835592 | tf_op jit(solution)/shard_map/ppermute | solution.py:328
  32.7 18.0 %collective-permute-start.4 = (f32[4,128,256]{2,1,0:T(8,128)S(1)}, f32[4,128,256]{2,1,0:T(8,128)S(1)}, u32[]{:S(2)}, u32[]{:S(2)}) collective-permute-start(f32[4,128,256]{2,1,0:T(8,128)S(1)} %get-tuple-element.26), channel_id=1, source_target_pairs={{0,1},{1,2},{2,3},{3,4},{4,5},{5,6},{6,7},{8,9},{9,10},{10,11},{11... | collective-permute-start | bytes 1572872 | tf_op jit(solution)/shard_map/ppermute | solution.py:328
  35.9 5.3 %collective-permute-start.5 = (f32[8,384]{1,0:T(8,128)S(1)}, f32[8,384]{1,0:T(8,128)S(1)}, u32[]{:S(2)}, u32[]{:S(2)}) collective-permute-start(f32[8,384]{1,0:T(8,128)S(1)} %get-tuple-element.27), channel_id=1, source_target_pairs={{1,0},{2,1},{3,2},{4,3},{5,4},{6,5},{7,6},{9,8},{10,9},{11,10},{12... | collective-permute-start | bytes 36872 | tf_op jit(solution)/shard_map/ppermute | solution.py:328
  41.3 12.6 %collective-permute-start.7 = (f32[4,128,128]{2,1,0:T(8,128)S(1)}, f32[4,128,128]{2,1,0:T(8,128)S(1)}, u32[]{:S(2)}, u32[]{:S(2)}) collective-permute-start(f32[4,128,128]{2,1,0:T(8,128)S(1)} %get-tuple-element.31), channel_id=1, source_target_pairs={{0,8},{1,9},{2,10},{3,11},{4,12},{5,13},{6,14},{7,15},{8,16},{9,17... | collective-permute-start | bytes 786440 | tf_op jit(solution)/shard_map/ppermute | solution.py:328
  43.2 7.4 %collective-permute-start.8 = (f32[8,128]{1,0:T(8,128)S(1)}, f32[8,128]{1,0:T(8,128)S(1)}, u32[]{:S(2)}, u32[]{:S(2)}) collective-permute-start(f32[8,128]{1,0:T(8,128)S(1)} %get-tuple-element.32), channel_id=1, source_target_pairs={{8,0},{9,1},{10,2},{11,3},{12,4},{13,5},{14,6},{15,7},{16,8},{17,9... | collective-permute-start | bytes 12296 | tf_op jit(solution)/shard_map/ppermute | solution.py:328
